TPU v7x, 32 devices: a whole 2x2x4 slice. The times are simulated.
32 devices in a mesh: lon: 8 (over y, x, core), lat: 4 (over z).
Axes of the slice: x: 2, y: 2, z: 4, core: 2. Of those that a mesh axis runs over, the one named last changes fastest.
Arguments:
- tracer: float32 [4096, 4096], P('lon', 'lat'), parts along dimension 1, may hold values from -7 to 7
- lower2: float32 [4096, 4096], P('lon', 'lat'), parts along dimension 1, may hold values from -4096 to -256
- lower1: float32 [4096, 4096], P('lon', 'lat'), parts along dimension 1, may hold values from -6144 to -256
- upper1: float32 [4096, 4096], P('lon', 'lat'), parts along dimension 1, may hold values from -4096 to -128
- upper2: float32 [4096, 4096], P('lon', 'lat'), parts along dimension 1, may hold values from -2048 to -64
Outputs:
- advanced: float32 [4096, 4096], P('lon', 'lat'), parts along dimension 1
There are 4 independent parts, one for each index of `lat`. A program takes and returns all parts, laid end to end along the dimension named above; each array names one. Nothing has to cross between parts.
All inputs are finite; a program needn't handle non-finite values.
Results may differ from a plain program's by a relative error of at most 0.0003.
Values sent between devices are 32-bit elements; how exact they have to be, the bound alone decides.
A program may use at most 128 MiB of HBM per device.

v0:
```python
import functools

import jax
import jax.numpy as jnp
from jax import lax
from jax.experimental import pallas as pl
from jax.experimental.pallas import tpu as pltpu
from jax.sharding import PartitionSpec as P

SUB = 8
LANE = 128
SENT = 24
BACK = 8
GROUP = 4
F32 = jnp.float32


def unpack(piece):
    return piece[0:2], piece[2:6], piece[6:10], piece[10:12], piece[12:16], piece[16:20]


def mat_vec(m, v):
    return (m[0] * v[0] + m[1] * v[1], m[2] * v[0] + m[3] * v[1])


def mat_mat(m, k):
    return (
        m[0] * k[0] + m[1] * k[2],
        m[0] * k[1] + m[1] * k[3],
        m[2] * k[0] + m[3] * k[2],
        m[2] * k[1] + m[3] * k[3],
    )


def plus(a, b):
    return tuple(x + y for x, y in zip(a, b))


def inverse(m):
    scale = 1.0 / (m[0] * m[3] - m[1] * m[2])
    return (m[3] * scale, -(m[1] * scale), -(m[2] * scale), m[0] * scale)


def interface(west, east, constant_only=False):
    _, _, _, lc, le, lw = unpack(west)
    fc, fe, fw, _, _, _ = unpack(east)
    loop = mat_mat(fw, le)
    inv = inverse((1.0 - loop[0], -loop[1], -loop[2], 1.0 - loop[3]))
    first_c = mat_vec(inv, plus(fc, mat_vec(fw, lc)))
    last_c = plus(lc, mat_vec(le, first_c))
    if constant_only:
        return first_c, last_c
    first_e = mat_mat(inv, fe)
    first_w = mat_mat(inv, mat_mat(fw, lw))
    last_e = mat_mat(le, first_e)
    last_w = plus(lw, mat_mat(le, first_w))
    return first_c, first_e, first_w, last_c, last_e, last_w


def joined(west, east):
    first_c, first_e, first_w, last_c, last_e, last_w = interface(west, east)
    fc, fe, fw, _, _, _ = unpack(west)
    _, _, _, lc, le, lw = unpack(east)
    return (
        plus(fc, mat_vec(fe, first_c))
        + mat_mat(fe, first_e)
        + plus(fw, mat_mat(fe, first_w))
        + plus(lc, mat_vec(lw, last_c))
        + plus(le, mat_mat(lw, last_e))
        + mat_mat(lw, last_w)
    )


EMPTY = (0.0, 0.0, 1.0, 0.0, 0.0, 1.0, 0.0, 0.0, 0.0, 0.0) + (
    0.0, 0.0, 0.0, 0.0, 0.0, 0.0, 1.0, 0.0, 0.0, 1.0)


def moved(piece, by):
    count = piece[0].shape[0]
    place = lax.broadcasted_iota(jnp.int32, piece[0].shape, 0)
    inside = place >= by if by > 0 else place < count + by
    return tuple(
        jnp.where(inside, pltpu.roll(x, by % count, 0), blank) for x, blank in zip(piece, EMPTY)
    )


def suffixes(piece):
    step = 1
    while step < piece[0].shape[0]:
        piece = joined(piece, moved(piece, -step))
        step *= 2
    return piece


def prefixes_before(piece):
    piece = moved(piece, 1)
    step = 1
    while step < piece[0].shape[0]:
        piece = joined(moved(piece, step), piece)
        step *= 2
    return piece


def kernel(
    peers, t_hbm, l2_hbm, l1_hbm, u1_hbm, u2_hbm, z_hbm,
    t_s, l2_s, l1_s, u1_s, u2_s, z_s, p_s, q_s, g_s, wa_s, wb_s,
    piece_s, inner_s, send_s, recv_s, back_s, ret_s,
    in_sem, out_sem, send_sem, recv_sem, back_send_sem, back_recv_sem,
):
    rows, lines = t_hbm.shape
    tiles = lines // LANE
    length = rows // SUB
    group = min(GROUP, tiles)
    me = lax.axis_index("lon")
    others = [lax.rem(me + k, peers) for k in range(1, peers)]

    def owning(who, action):
        if tiles < peers:
            pl.when(who < tiles)(action)
        else:
            action()

    def loads(tile):
        pairs = ((t_hbm, t_s), (l2_hbm, l2_s), (l1_hbm, l1_s), (u1_hbm, u1_s), (u2_hbm, u2_s))
        return [
            pltpu.make_async_copy(
                src.at[:, pl.ds(tile * LANE, LANE)],
                dst.at[pl.ds(tile * rows, rows), :],
                in_sem.at[idx, tile],
            )
            for idx, (src, dst) in enumerate(pairs)
        ]

    for tile in range(tiles):
        for copy in loads(tile):
            copy.start()

    barrier = pltpu.get_barrier_semaphore()
    for peer in others:
        pl.semaphore_signal(
            barrier, inc=1, device_id={"lon": peer}, device_id_type=pl.DeviceIdType.MESH
        )

    ret_s[0] = jnp.zeros((SUB, LANE), F32)
    back_s[pl.ds(0, SUB), :] = jnp.ones((SUB, LANE), F32)
    zero = ret_s[0]
    one = back_s[pl.ds(0, SUB), :]

    def strided(tile, row):
        return pl.ds(tile * rows + row, SUB, stride=length)

    def packed(tile):
        return pl.ds(tile * SUB, SUB)

    for base in range(0, tiles, group):
        members = list(range(base, base + group))
        for tile in members:
            for copy in loads(tile):
                copy.wait()

        def forward(i, state, members=members):
            new_state = []
            for tile, (p1, q1, g1, a1, b1, p2, q2, g2, a2, b2) in zip(members, state):
                here = strided(tile, i)
                l2, l1, u1, u2 = l2_s[here, :], l1_s[here, :], u1_s[here, :], u2_s[here, :]
                target = t_s[here, :]
                centre = 1.0 + (jnp.abs(l2) + jnp.abs(l1) + jnp.abs(u1) + jnp.abs(u2))
                beta = l1 - l2 * p2
                scale = 1.0 / ((centre - l2 * q2) - beta * p1)
                p0 = (u1 - beta * q1) * scale
                q0 = u2 * scale
                far = l2 * scale
                near = beta * scale
                g0 = (target * scale - far * g2) - near * g1
                a0 = -(far * a2 + near * a1)
                b0 = -(far * b2 + near * b1)
                at = packed(tile)
                p_s[i, at, :] = p0
                q_s[i, at, :] = q0
                g_s[i, at, :] = g0
                wa_s[i, at, :] = a0
                wb_s[i, at, :] = b0
                new_state.append((p0, q0, g0, a0, b0, p1, q1, g1, a1, b1))
            return tuple(new_state)

        start = (zero, zero, zero, zero, -one, zero, zero, zero, -one, zero)
        ends = lax.fori_loop(0, length, forward, (start,) * group, unroll=2)

        def first_rows(i, state, members=members):
            new_state = []
            for tile, forms in zip(members, state):
                at = packed(tile)
                p, q, g = p_s[i, at, :], q_s[i, at, :], g_s[i, at, :]
                wa, wb = wa_s[i, at, :], wb_s[i, at, :]
                new_forms = []
                for c, x, y, a, b in forms:
                    new_forms.append((c + x * g, y - x * p, -(x * q), a - x * wa, b - x * wb))
                new_state.append(tuple(new_forms))
            return tuple(new_state)

        forms = ((zero, one, zero, zero, zero), (zero, zero, one, zero, zero))
        firsts = lax.fori_loop(0, length, first_rows, (forms,) * group, unroll=2)

        for tile, end, (f0, f1) in zip(members, ends, firsts):
            p1, q1, g1, a1, b1, p2, q2, g2, a2, b2 = end
            piece = (
                f0[0], f1[0],
                f0[1], f0[2], f1[1], f1[2],
                f0[3], f0[4], f1[3], f1[4],
                g2 - p2 * g1, g1,
                p2 * p1 - q2, p2 * q1, -p1, -q1,
                p2 * a1 - a2, p2 * b1 - b2, -a1, -b1,
            )
            for idx, value in enumerate(piece):
                piece_s[tile, pl.ds(idx * SUB, SUB), :] = value

    def stored(tile):
        return tuple(piece_s[tile, pl.ds(idx * SUB, SUB), :] for idx in range(20))

    def whole(tile, carry):
        total = suffixes(stored(tile))
        for idx, value in enumerate(total):
            inner_s[tile, pl.ds(idx * SUB, SUB), :] = value
            send_s[tile, pl.ds(idx, 1), :] = value[0:1, :]
        return carry

    lax.fori_loop(0, tiles, whole, 0)

    def outward(peer, source):
        return pltpu.make_async_remote_copy(
            src_ref=send_s.at[peer],
            dst_ref=recv_s.at[pl.ds(pl.multiple_of(source * SENT, SENT), SENT), :],
            send_sem=send_sem.at[peer],
            recv_sem=recv_sem.at[source],
            device_id={"lon": peer},
            device_id_type=pl.DeviceIdType.MESH,
        )

    def homeward(peer, source):
        return pltpu.make_async_remote_copy(
            src_ref=back_s.at[pl.ds(pl.multiple_of(peer * BACK, BACK), BACK), :],
            dst_ref=ret_s.at[source],
            send_sem=back_send_sem.at[peer],
            recv_sem=back_recv_sem.at[source],
            device_id={"lon": peer},
            device_id_type=pl.DeviceIdType.MESH,
        )

    pl.semaphore_wait(barrier, peers - 1)
    for peer in others:
        owning(peer, lambda peer=peer: outward(peer, me).start())

    def inside(tile, carry):
        total = tuple(inner_s[tile, pl.ds(idx * SUB, SUB), :] for idx in range(20))
        parts = interface(prefixes_before(stored(tile)), total)
        for idx, value in enumerate(sum(parts, ())):
            inner_s[tile, pl.ds(idx * SUB, SUB), :] = value
        return carry

    lax.fori_loop(0, tiles, inside, 0)

    def solve_lines():
        recv_s[pl.ds(pl.multiple_of(me * SENT, SENT), SENT), :] = send_s[me]
        for peer in others:
            outward(me, peer).wait_recv()
        segments = tuple(recv_s[pl.ds(idx, peers, stride=SENT), :] for idx in range(20))
        first, last = interface(prefixes_before(segments), suffixes(segments), True)
        place = lax.broadcasted_iota(jnp.int32, (peers, LANE), 0)
        east = [jnp.where(place < peers - 1, pltpu.roll(x, peers - 1, 0), 0.0) for x in first]
        west = [jnp.where(place > 0, x, 0.0) for x in last]
        for idx, value in enumerate(east + west):
            back_s[pl.ds(idx, peers, stride=BACK), :] = value
        for peer in others:
            homeward(peer, me).start()
        ret_s[me] = back_s[pl.ds(pl.multiple_of(me * BACK, BACK), BACK), :]

    owning(me, solve_lines)

    for peer in others:
        owning(peer, lambda peer=peer: homeward(me, peer).wait_recv())

    place = lax.broadcasted_iota(jnp.int32, (SUB, LANE), 0)

    def store(tile):
        return pltpu.make_async_copy(
            z_s.at[pl.ds(tile * rows, rows), :],
            z_hbm.at[:, pl.ds(tile * LANE, LANE)],
            out_sem.at[tile],
        )

    for base in range(0, tiles, group):
        members = list(range(base, base + group))
        start, bounds = [], []
        for tile in members:
            e0, e1, w0, w1 = (
                jnp.broadcast_to(ret_s[tile, pl.ds(idx, 1), :], (SUB, LANE)) for idx in range(4)
            )
            inner = tuple(inner_s[tile, pl.ds(idx * SUB, SUB), :] for idx in range(20))
            first = plus(plus(inner[0:2], mat_vec(inner[2:6], (e0, e1))), mat_vec(inner[6:10], (w0, w1)))
            last = plus(plus(inner[10:12], mat_vec(inner[12:16], (e0, e1))), mat_vec(inner[16:20], (w0, w1)))
            east = [
                jnp.where(place < SUB - 1, pltpu.roll(x, SUB - 1, 0), edge)
                for x, edge in zip(first, (e0, e1))
            ]
            start.append((east[0], east[1]))
            bounds.append(last)

        def backward(step, state, members=members, bounds=bounds):
            i = length - 1 - step
            new_state = []
            for tile, (wa, wb), (x1, x2) in zip(members, bounds, state):
                at = packed(tile)
                free = (g_s[i, at, :] - wa_s[i, at, :] * wa) - wb_s[i, at, :] * wb
                x0 = (free - q_s[i, at, :] * x2) - p_s[i, at, :] * x1
                z_s[strided(tile, i), :] = x0
                new_state.append((x0, x1))
            return tuple(new_state)

        lax.fori_loop(0, length, backward, tuple(start), unroll=2)
        for tile in members:
            store(tile).start()

    for tile in range(tiles):
        store(tile).wait()
    for peer in others:
        owning(peer, lambda peer=peer: outward(peer, me).wait_send())

    def sent_home():
        for peer in others:
            homeward(peer, me).wait_send()

    owning(me, sent_home)


def per_device(tracer, lower2, lower1, upper1, upper2):
    rows, lines = tracer.shape
    peers = lax.axis_size("lon")
    tiles = lines // LANE
    assert rows % (2 * SUB) == 0 and lines % LANE == 0 and tiles <= peers
    assert tiles % min(GROUP, tiles) == 0
    plane = pltpu.VMEM((tiles * rows, LANE), F32)
    factor = pltpu.VMEM((rows // SUB, tiles * SUB, LANE), F32)
    sem = pltpu.SemaphoreType.DMA
    solved = pl.pallas_call(
        functools.partial(kernel, peers),
        out_shape=jax.ShapeDtypeStruct((rows, lines), F32),
        in_specs=[pl.BlockSpec(memory_space=pl.ANY)] * 5,
        out_specs=pl.BlockSpec(memory_space=pl.ANY),
        scratch_shapes=[plane] * 6
        + [factor] * 5
        + [
            pltpu.VMEM((tiles, 20 * SUB, LANE), F32),
            pltpu.VMEM((tiles, 20 * SUB, LANE), F32),
            pltpu.VMEM((tiles, SENT, LANE), F32),
            pltpu.VMEM((peers * SENT, LANE), F32),
            pltpu.VMEM((peers * BACK, LANE), F32),
            pltpu.VMEM((tiles, BACK, LANE), F32),
            sem((5, tiles)),
            sem((tiles,)),
            sem((peers,)),
            sem((peers,)),
            sem((peers,)),
            sem((peers,)),
        ],
        compiler_params=pltpu.CompilerParams(
            collective_id=0, has_side_effects=True, vmem_limit_bytes=48 * 1024 * 1024
        ),
        cost_estimate=pl.CostEstimate(
            flops=90 * rows * lines, bytes_accessed=24 * rows * lines, transcendentals=0
        ),
    )(tracer, lower2, lower1, upper1, upper2)
    return 2.0 * solved - tracer


def solution(mesh):
    spec = P("lon", "lat")
    return jax.shard_map(
        per_device, mesh=mesh, in_specs=(spec,) * 5, out_specs=spec, check_vma=False
    )
```

profile of v0, /device:TPU:0, one launch (start us, length us, event | category | flops | bytes accessed | tf_op | source)
XLA Modules:
  0.0 28.9 jit_solution(15223050636545580131)
XLA Ops:
  0.0 0.0 copy-start
  0.0 1.6 %copy-done = f32[512,1024]{1,0:T(8,128)S(1)} copy-done((f32[512,1024]{1,0:T(8,128)S(1)}, f32[512,1024]{1,0:T(8,128)}, u32[]{:S(2)}) %copy-start) | copy-done | bytes 2097176
  1.6 25.4 %shard_map.55 = f32[512,1024]{1,0:T(8,128)S(1)} custom-call(f32[512,1024]{1,0:T(8,128)S(1)} %copy-done, f32[512,1024]{1,0:T(8,128)} %l2_hbm.1, f32[512,1024]{1,0:T(8,128)} %l1_hbm.1, f32[512,1024]{1,0:T(8,128)} %u1_hbm.1, f32[512,1024]{1,0:T(8,128)} %u2_hbm.1), custom_call_target="tpu_custom_call" | custom-call | flops 47185920 | bytes 12582912 | tf_op jit(solution)/shard_map/pallas_call | solution.py:344
  27.0 1.9 %multiply_subtract_fusion = f32[512,1024]{1,0:T(8,128)} fusion(f32[512,1024]{1,0:T(8,128)S(1)} %copy-done, f32[512,1024]{1,0:T(8,128)S(1)} %shard_map.55), kind=kLoop, calls=%fused_computation | loop fusion | flops 1048576 | bytes 6291456 | tf_op jit(solution)/shard_map/sub | solution.py:372
Async XLA Ops:
  0.0 1.6 %copy-start = (f32[512,1024]{1,0:T(8,128)S(1)}, f32[512,1024]{1,0:T(8,128)}, u32[]{:S(2)}) copy-start(f32[512,1024]{1,0:T(8,128)} %t_hbm.1) | copy-start | bytes 6291460
where the time goes:
time: 29 us; the launch traced here: 28.9 us
  Pallas kernels  25.4 us (88%)
  other arithmetic  1.94 us (7%)
  local copies, waits for them, and re-layouts  1.59 us (5%)
    pallas_call x1, Pallas kernels, per_device(): pl.pallas_call(functools.partial(kernel, peers), out_shape=jax.ShapeDtype...  25.4 us
    sub x1, other arithmetic, per_device(): return 2.0 * solved - tracer  1.94 us
    unnamed x2, local copies, waits for them, and re-layouts  1.59 us

commit v1 on v0

--- a/solution.py
+++ b/solution.py
@@ -107,9 +107,9 @@
     piece_s, inner_s, send_s, recv_s, back_s, ret_s,
     in_sem, out_sem, send_sem, recv_sem, back_send_sem, back_recv_sem,
 ):
-    rows, lines = t_hbm.shape
+    _, length, lines = t_hbm.shape
     tiles = lines // LANE
-    length = rows // SUB
+    pitch = t_s.shape[1]
     group = min(GROUP, tiles)
     me = lax.axis_index("lon")
     others = [lax.rem(me + k, peers) for k in range(1, peers)]
@@ -124,12 +124,17 @@
         pairs = ((t_hbm, t_s), (l2_hbm, l2_s), (l1_hbm, l1_s), (u1_hbm, u1_s), (u2_hbm, u2_s))
         return [
             pltpu.make_async_copy(
-                src.at[:, pl.ds(tile * LANE, LANE)],
-                dst.at[pl.ds(tile * rows, rows), :],
+                src.at[:, :, pl.ds(tile * LANE, LANE)],
+                dst.at[pl.ds(tile * SUB, SUB), pl.ds(0, length), :],
                 in_sem.at[idx, tile],
             )
             for idx, (src, dst) in enumerate(pairs)
         ]
+
+    flat_rows = tiles * SUB * pitch
+    t_f, l2_f, l1_f, u1_f, u2_f, z_f = (
+        ref.reshape(flat_rows, LANE) for ref in (t_s, l2_s, l1_s, u1_s, u2_s, z_s)
+    )
 
     for tile in range(tiles):
         for copy in loads(tile):
@@ -147,7 +152,7 @@
     one = back_s[pl.ds(0, SUB), :]
 
     def strided(tile, row):
-        return pl.ds(tile * rows + row, SUB, stride=length)
+        return pl.ds(tile * SUB * pitch + row, SUB, stride=pitch)
 
     def packed(tile):
         return pl.ds(tile * SUB, SUB)
@@ -162,11 +167,11 @@
             new_state = []
             for tile, (p1, q1, g1, a1, b1, p2, q2, g2, a2, b2) in zip(members, state):
                 here = strided(tile, i)
-                l2, l1, u1, u2 = l2_s[here, :], l1_s[here, :], u1_s[here, :], u2_s[here, :]
-                target = t_s[here, :]
+                l2, l1, u1, u2 = l2_f[here, :], l1_f[here, :], u1_f[here, :], u2_f[here, :]
+                target = t_f[here, :]
                 centre = 1.0 + (jnp.abs(l2) + jnp.abs(l1) + jnp.abs(u1) + jnp.abs(u2))
                 beta = l1 - l2 * p2
-                scale = 1.0 / ((centre - l2 * q2) - beta * p1)
+                scale = pl.reciprocal((centre - l2 * q2) - beta * p1, approx=True)
                 p0 = (u1 - beta * q1) * scale
                 q0 = u2 * scale
                 far = l2 * scale
@@ -224,7 +229,7 @@
             send_s[tile, pl.ds(idx, 1), :] = value[0:1, :]
         return carry
 
-    lax.fori_loop(0, tiles, whole, 0)
+    lax.fori_loop(0, tiles, whole, 0, unroll=2)
 
     def outward(peer, source):
         return pltpu.make_async_remote_copy(
@@ -257,7 +262,7 @@
             inner_s[tile, pl.ds(idx * SUB, SUB), :] = value
         return carry
 
-    lax.fori_loop(0, tiles, inside, 0)
+    lax.fori_loop(0, tiles, inside, 0, unroll=2)
 
     def solve_lines():
         recv_s[pl.ds(pl.multiple_of(me * SENT, SENT), SENT), :] = send_s[me]
@@ -283,8 +288,8 @@
 
     def store(tile):
         return pltpu.make_async_copy(
-            z_s.at[pl.ds(tile * rows, rows), :],
-            z_hbm.at[:, pl.ds(tile * LANE, LANE)],
+            z_s.at[pl.ds(tile * SUB, SUB), pl.ds(0, length), :],
+            z_hbm.at[:, :, pl.ds(tile * LANE, LANE)],
             out_sem.at[tile],
         )
 
@@ -312,7 +317,7 @@
                 at = packed(tile)
                 free = (g_s[i, at, :] - wa_s[i, at, :] * wa) - wb_s[i, at, :] * wb
                 x0 = (free - q_s[i, at, :] * x2) - p_s[i, at, :] * x1
-                z_s[strided(tile, i), :] = x0
+                z_f[strided(tile, i), :] = 2.0 * x0 - t_f[strided(tile, i), :]
                 new_state.append((x0, x1))
             return tuple(new_state)
 
@@ -336,14 +341,16 @@
     rows, lines = tracer.shape
     peers = lax.axis_size("lon")
     tiles = lines // LANE
-    assert rows % (2 * SUB) == 0 and lines % LANE == 0 and tiles <= peers
+    assert rows % (SUB * SUB) == 0 and lines % LANE == 0 and tiles <= peers
     assert tiles % min(GROUP, tiles) == 0
-    plane = pltpu.VMEM((tiles * rows, LANE), F32)
-    factor = pltpu.VMEM((rows // SUB, tiles * SUB, LANE), F32)
+    length = rows // SUB
+    pitch = length if length % (2 * SUB) else length + SUB
+    plane = pltpu.VMEM((tiles * SUB, pitch, LANE), F32)
+    factor = pltpu.VMEM((length, tiles * SUB, LANE), F32)
     sem = pltpu.SemaphoreType.DMA
     solved = pl.pallas_call(
         functools.partial(kernel, peers),
-        out_shape=jax.ShapeDtypeStruct((rows, lines), F32),
+        out_shape=jax.ShapeDtypeStruct((SUB, length, lines), F32),
         in_specs=[pl.BlockSpec(memory_space=pl.ANY)] * 5,
         out_specs=pl.BlockSpec(memory_space=pl.ANY),
         scratch_shapes=[plane] * 6
@@ -363,13 +370,13 @@
             sem((peers,)),
         ],
         compiler_params=pltpu.CompilerParams(
-            collective_id=0, has_side_effects=True, vmem_limit_bytes=48 * 1024 * 1024
+            collective_id=0, has_side_effects=True, vmem_limit_bytes=60 * 1024 * 1024
         ),
         cost_estimate=pl.CostEstimate(
             flops=90 * rows * lines, bytes_accessed=24 * rows * lines, transcendentals=0
         ),
-    )(tracer, lower2, lower1, upper1, upper2)
-    return 2.0 * solved - tracer
+    )(*(x.reshape(SUB, length, lines) for x in (tracer, lower2, lower1, upper1, upper2)))
+    return solved.reshape(rows, lines)
 
 
 def solution(mesh):

time: 29 us -> 24.4 us (0.84)
  Pallas kernels: 25.4 us -> 21.1 us
  other arithmetic: 1.94 us -> 0 us
  local copies, waits for them, and re-layouts: 1.59 us -> 3.16 us
    pallas_call x1, Pallas kernels: 25.4 us -> 21.1 us  [per_device(): pl.pallas_call(functools.partial(kernel, peers), out_shape=jax.ShapeDtype...]
    sub x1 -> x0, other arithmetic: 1.94 us -> none  [per_device(): return 2.0 * solved - tracer]
    unnamed x2 -> x1, local copies, waits for them, and re-layouts: 1.59 us -> 3.16 us
where the time goes in v1:
time: 24.4 us; the launch traced here: 24.2 us
  Pallas kernels  21.1 us (86%)
  local copies, waits for them, and re-layouts  3.16 us (13%)
    pallas_call x1, Pallas kernels, per_device(): pl.pallas_call(functools.partial(kernel, peers), out_shape=jax.ShapeDtype...  21.1 us
    unnamed x1, local copies, waits for them, and re-layouts  3.16 us

profile of v1, /device:TPU:0, one launch (start us, length us, event | category | flops | bytes accessed | tf_op | source)
XLA Modules:
  0.0 24.2 jit_solution(17772653031878612270)
XLA Ops:
  0.0 21.1 %shard_map.55 = f32[8,64,1024]{2,1,0:T(8,128)} custom-call(f32[8,64,1024]{2,1,0:T(8,128)} %bitcast.7, f32[8,64,1024]{2,1,0:T(8,128)} %bitcast.8, f32[8,64,1024]{2,1,0:T(8,128)} %bitcast.9, f32[8,64,1024]{2,1,0:T(8,128)} %bitcast.10, f32[8,64,1024]{2,1,0:T(8,128)} %bitcast.11), custom_call_target="tpu_custom_call" | custom-call | flops 47185920 | bytes 12582912 | tf_op jit(solution)/shard_map/pallas_call | solution.py:351
  21.1 3.2 %copy.7 = f32[512,1024]{1,0:T(8,128)} copy(f32[512,1024]{1,0:T(8,128)} %bitcast.6) | data formatting | bytes 4194304

commit v2 on v1

--- a/solution.py
+++ b/solution.py
@@ -12,6 +12,8 @@
 SENT = 24
 BACK = 8
 GROUP = 4
+PARTS = 2
+LEVELS = 3
 F32 = jnp.float32
 
 
@@ -58,10 +60,11 @@
 
 
 def joined(west, east):
-    first_c, first_e, first_w, last_c, last_e, last_w = interface(west, east)
+    meet = interface(west, east)
+    first_c, first_e, first_w, last_c, last_e, last_w = meet
     fc, fe, fw, _, _, _ = unpack(west)
     _, _, _, lc, le, lw = unpack(east)
-    return (
+    piece = (
         plus(fc, mat_vec(fe, first_c))
         + mat_mat(fe, first_e)
         + plus(fw, mat_mat(fe, first_w))
@@ -69,36 +72,27 @@
         + plus(le, mat_mat(lw, last_e))
         + mat_mat(lw, last_w)
     )
-
-
-EMPTY = (0.0, 0.0, 1.0, 0.0, 0.0, 1.0, 0.0, 0.0, 0.0, 0.0) + (
-    0.0, 0.0, 0.0, 0.0, 0.0, 0.0, 1.0, 0.0, 0.0, 1.0)
-
-
-def moved(piece, by):
-    count = piece[0].shape[0]
-    place = lax.broadcasted_iota(jnp.int32, piece[0].shape, 0)
-    inside = place >= by if by > 0 else place < count + by
-    return tuple(
-        jnp.where(inside, pltpu.roll(x, by % count, 0), blank) for x, blank in zip(piece, EMPTY)
-    )
-
-
-def suffixes(piece):
-    step = 1
-    while step < piece[0].shape[0]:
-        piece = joined(piece, moved(piece, -step))
-        step *= 2
-    return piece
-
-
-def prefixes_before(piece):
-    piece = moved(piece, 1)
-    step = 1
-    while step < piece[0].shape[0]:
-        piece = joined(moved(piece, step), piece)
-        step *= 2
-    return piece
+    return piece, sum(meet, ())
+
+
+def rolled(values, by):
+    count = values[0].shape[0]
+    return tuple(pltpu.roll(x, by % count, 0) for x in values)
+
+
+def split_pairs(meet, east, west, step):
+    first = plus(plus(meet[0:2], mat_vec(meet[2:6], east)), mat_vec(meet[6:10], west))
+    last = plus(plus(meet[10:12], mat_vec(meet[12:16], east)), mat_vec(meet[16:20], west))
+    count = first[0].shape[0]
+    place = lax.broadcasted_iota(jnp.int32, first[0].shape, 0)
+    lower = lax.rem(place, 2 * step) < step
+    if 2 * step < count:
+        east = rolled(east, step)
+    moved = rolled(last, step)
+    return (
+        tuple(jnp.where(lower, a, b) for a, b in zip(first, east)),
+        tuple(jnp.where(lower, a, b) for a, b in zip(west, moved)),
+    )
 
 
 def kernel(
@@ -120,13 +114,14 @@
         else:
             action()
 
-    def loads(tile):
+    def loads(tile, part):
         pairs = ((t_hbm, t_s), (l2_hbm, l2_s), (l1_hbm, l1_s), (u1_hbm, u1_s), (u2_hbm, u2_s))
+        some = pl.ds(part * (length // PARTS), length // PARTS)
         return [
             pltpu.make_async_copy(
-                src.at[:, :, pl.ds(tile * LANE, LANE)],
-                dst.at[pl.ds(tile * SUB, SUB), pl.ds(0, length), :],
-                in_sem.at[idx, tile],
+                src.at[:, some, pl.ds(tile * LANE, LANE)],
+                dst.at[pl.ds(tile * SUB, SUB), some, :],
+                in_sem.at[idx, tile, part],
             )
             for idx, (src, dst) in enumerate(pairs)
         ]
@@ -136,9 +131,11 @@
         ref.reshape(flat_rows, LANE) for ref in (t_s, l2_s, l1_s, u1_s, u2_s, z_s)
     )
 
-    for tile in range(tiles):
-        for copy in loads(tile):
-            copy.start()
+    for base in range(0, tiles, group):
+        for part in range(PARTS):
+            for tile in range(base, base + group):
+                for copy in loads(tile, part):
+                    copy.start()
 
     barrier = pltpu.get_barrier_semaphore()
     for peer in others:
@@ -159,26 +156,22 @@
 
     for base in range(0, tiles, group):
         members = list(range(base, base + group))
-        for tile in members:
-            for copy in loads(tile):
-                copy.wait()
-
         def forward(i, state, members=members):
             new_state = []
             for tile, (p1, q1, g1, a1, b1, p2, q2, g2, a2, b2) in zip(members, state):
                 here = strided(tile, i)
                 l2, l1, u1, u2 = l2_f[here, :], l1_f[here, :], u1_f[here, :], u2_f[here, :]
                 target = t_f[here, :]
-                centre = 1.0 + (jnp.abs(l2) + jnp.abs(l1) + jnp.abs(u1) + jnp.abs(u2))
-                beta = l1 - l2 * p2
+                centre = (l2 + l1 + u1 + u2) - 1.0
+                beta = l1 + l2 * p2
                 scale = pl.reciprocal((centre - l2 * q2) - beta * p1, approx=True)
-                p0 = (u1 - beta * q1) * scale
+                p0 = (u1 + beta * q1) * scale
                 q0 = u2 * scale
                 far = l2 * scale
                 near = beta * scale
-                g0 = (target * scale - far * g2) - near * g1
-                a0 = -(far * a2 + near * a1)
-                b0 = -(far * b2 + near * b1)
+                g0 = (far * g2 - target * scale) + near * g1
+                a0 = far * a2 + near * a1
+                b0 = far * b2 + near * b1
                 at = packed(tile)
                 p_s[i, at, :] = p0
                 q_s[i, at, :] = q0
@@ -188,8 +181,14 @@
                 new_state.append((p0, q0, g0, a0, b0, p1, q1, g1, a1, b1))
             return tuple(new_state)
 
-        start = (zero, zero, zero, zero, -one, zero, zero, zero, -one, zero)
-        ends = lax.fori_loop(0, length, forward, (start,) * group, unroll=2)
+        start = (zero, zero, zero, zero, one, zero, zero, zero, one, zero)
+        ends = (start,) * group
+        for part in range(PARTS):
+            for tile in members:
+                for copy in loads(tile, part):
+                    copy.wait()
+            span = length // PARTS
+            ends = lax.fori_loop(part * span, (part + 1) * span, forward, ends, unroll=2)
 
         def first_rows(i, state, members=members):
             new_state = []
@@ -199,7 +198,7 @@
                 wa, wb = wa_s[i, at, :], wb_s[i, at, :]
                 new_forms = []
                 for c, x, y, a, b in forms:
-                    new_forms.append((c + x * g, y - x * p, -(x * q), a - x * wa, b - x * wb))
+                    new_forms.append((c + x * g, y + x * p, x * q, a + x * wa, b + x * wb))
                 new_state.append(tuple(new_forms))
             return tuple(new_state)
 
@@ -212,20 +211,20 @@
                 f0[0], f1[0],
                 f0[1], f0[2], f1[1], f1[2],
                 f0[3], f0[4], f1[3], f1[4],
-                g2 - p2 * g1, g1,
-                p2 * p1 - q2, p2 * q1, -p1, -q1,
-                p2 * a1 - a2, p2 * b1 - b2, -a1, -b1,
+                g2 + p2 * g1, g1,
+                p2 * p1 + q2, p2 * q1, p1, q1,
+                p2 * a1 + a2, p2 * b1 + b2, a1, b1,
             )
             for idx, value in enumerate(piece):
                 piece_s[tile, pl.ds(idx * SUB, SUB), :] = value
 
-    def stored(tile):
-        return tuple(piece_s[tile, pl.ds(idx * SUB, SUB), :] for idx in range(20))
-
     def whole(tile, carry):
-        total = suffixes(stored(tile))
-        for idx, value in enumerate(total):
-            inner_s[tile, pl.ds(idx * SUB, SUB), :] = value
+        piece = tuple(piece_s[tile, pl.ds(idx * SUB, SUB), :] for idx in range(20))
+        for level in range(LEVELS):
+            piece, meet = joined(piece, rolled(piece, -(1 << level)))
+            for idx, value in enumerate(meet):
+                inner_s[tile, pl.ds((level * 20 + idx) * SUB, SUB), :] = value
+        for idx, value in enumerate(piece):
             send_s[tile, pl.ds(idx, 1), :] = value[0:1, :]
         return carry
 
@@ -255,24 +254,24 @@
     for peer in others:
         owning(peer, lambda peer=peer: outward(peer, me).start())
 
-    def inside(tile, carry):
-        total = tuple(inner_s[tile, pl.ds(idx * SUB, SUB), :] for idx in range(20))
-        parts = interface(prefixes_before(stored(tile)), total)
-        for idx, value in enumerate(sum(parts, ())):
-            inner_s[tile, pl.ds(idx * SUB, SUB), :] = value
-        return carry
-
-    lax.fori_loop(0, tiles, inside, 0, unroll=2)
-
     def solve_lines():
         recv_s[pl.ds(pl.multiple_of(me * SENT, SENT), SENT), :] = send_s[me]
         for peer in others:
             outward(me, peer).wait_recv()
-        segments = tuple(recv_s[pl.ds(idx, peers, stride=SENT), :] for idx in range(20))
-        first, last = interface(prefixes_before(segments), suffixes(segments), True)
+        piece = tuple(recv_s[pl.ds(idx, peers, stride=SENT), :] for idx in range(20))
+        meets = []
+        step = 1
+        while 2 * step < peers:
+            piece, meet = joined(piece, rolled(piece, -step))
+            meets.append(meet)
+            step *= 2
+        first, last = interface(piece, rolled(piece, -step), True)
         place = lax.broadcasted_iota(jnp.int32, (peers, LANE), 0)
-        east = [jnp.where(place < peers - 1, pltpu.roll(x, peers - 1, 0), 0.0) for x in first]
-        west = [jnp.where(place > 0, x, 0.0) for x in last]
+        east = tuple(jnp.where(place < step, x, 0.0) for x in first)
+        west = tuple(jnp.where(place < step, 0.0, x) for x in rolled(last, step))
+        for meet in reversed(meets):
+            step //= 2
+            east, west = split_pairs(meet, east, west, step)
         for idx, value in enumerate(east + west):
             back_s[pl.ds(idx, peers, stride=BACK), :] = value
         for peer in others:
@@ -283,8 +282,6 @@
 
     for peer in others:
         owning(peer, lambda peer=peer: homeward(me, peer).wait_recv())
-
-    place = lax.broadcasted_iota(jnp.int32, (SUB, LANE), 0)
 
     def store(tile):
         return pltpu.make_async_copy(
@@ -300,23 +297,22 @@
             e0, e1, w0, w1 = (
                 jnp.broadcast_to(ret_s[tile, pl.ds(idx, 1), :], (SUB, LANE)) for idx in range(4)
             )
-            inner = tuple(inner_s[tile, pl.ds(idx * SUB, SUB), :] for idx in range(20))
-            first = plus(plus(inner[0:2], mat_vec(inner[2:6], (e0, e1))), mat_vec(inner[6:10], (w0, w1)))
-            last = plus(plus(inner[10:12], mat_vec(inner[12:16], (e0, e1))), mat_vec(inner[16:20], (w0, w1)))
-            east = [
-                jnp.where(place < SUB - 1, pltpu.roll(x, SUB - 1, 0), edge)
-                for x, edge in zip(first, (e0, e1))
-            ]
-            start.append((east[0], east[1]))
-            bounds.append(last)
+            east, west = (e0, e1), (w0, w1)
+            for level in reversed(range(LEVELS)):
+                meet = tuple(
+                    inner_s[tile, pl.ds((level * 20 + idx) * SUB, SUB), :] for idx in range(20)
+                )
+                east, west = split_pairs(meet, east, west, 1 << level)
+            start.append(east)
+            bounds.append(west)
 
         def backward(step, state, members=members, bounds=bounds):
             i = length - 1 - step
             new_state = []
             for tile, (wa, wb), (x1, x2) in zip(members, bounds, state):
                 at = packed(tile)
-                free = (g_s[i, at, :] - wa_s[i, at, :] * wa) - wb_s[i, at, :] * wb
-                x0 = (free - q_s[i, at, :] * x2) - p_s[i, at, :] * x1
+                free = (g_s[i, at, :] + wa_s[i, at, :] * wa) + wb_s[i, at, :] * wb
+                x0 = (free + q_s[i, at, :] * x2) + p_s[i, at, :] * x1
                 z_f[strided(tile, i), :] = 2.0 * x0 - t_f[strided(tile, i), :]
                 new_state.append((x0, x1))
             return tuple(new_state)
@@ -341,7 +337,7 @@
     rows, lines = tracer.shape
     peers = lax.axis_size("lon")
     tiles = lines // LANE
-    assert rows % (SUB * SUB) == 0 and lines % LANE == 0 and tiles <= peers
+    assert rows % (PARTS * SUB * SUB) == 0 and peers & (peers - 1) == 0 and lines % LANE == 0 and tiles <= peers
     assert tiles % min(GROUP, tiles) == 0
     length = rows // SUB
     pitch = length if length % (2 * SUB) else length + SUB
@@ -357,12 +353,12 @@
         + [factor] * 5
         + [
             pltpu.VMEM((tiles, 20 * SUB, LANE), F32),
-            pltpu.VMEM((tiles, 20 * SUB, LANE), F32),
+            pltpu.VMEM((tiles, LEVELS * 20 * SUB, LANE), F32),
             pltpu.VMEM((tiles, SENT, LANE), F32),
             pltpu.VMEM((peers * SENT, LANE), F32),
             pltpu.VMEM((peers * BACK, LANE), F32),
             pltpu.VMEM((tiles, BACK, LANE), F32),
-            sem((5, tiles)),
+            sem((5, tiles, PARTS)),
             sem((tiles,)),
             sem((peers,)),
             sem((peers,)),
@@ -370,7 +366,7 @@
             sem((peers,)),
         ],
         compiler_params=pltpu.CompilerParams(
-            collective_id=0, has_side_effects=True, vmem_limit_bytes=60 * 1024 * 1024
+            collective_id=0, has_side_effects=True, vmem_limit_bytes=50 * 1024 * 1024
         ),
         cost_estimate=pl.CostEstimate(
             flops=90 * rows * lines, bytes_accessed=24 * rows * lines, transcendentals=0

time: 24.4 us -> 20.9 us (0.86)
  local copies, waits for them, and re-layouts: 3.16 us -> 1.32 us
  Pallas kernels: 21.1 us -> 19.4 us
    unnamed x1, local copies, waits for them, and re-layouts: 3.16 us -> 1.32 us
    pallas_call x1, Pallas kernels: 21.1 us -> 19.4 us  [per_device(): pl.pallas_call(functools.partial(kernel, peers), out_shape=jax.ShapeDtype...]
where the time goes in v2:
time: 20.9 us; the launch traced here: 20.7 us
  Pallas kernels  19.4 us (93%)
  local copies, waits for them, and re-layouts  1.32 us (6%)
    pallas_call x1, Pallas kernels, per_device(): pl.pallas_call(functools.partial(kernel, peers), out_shape=jax.ShapeDtype...  19.4 us
    unnamed x1, local copies, waits for them, and re-layouts  1.32 us

profile of v2, /device:TPU:0, one launch (start us, length us, event | category | flops | bytes accessed | tf_op | source)
XLA Modules:
  0.0 20.7 jit_solution(7516204677853293786)
XLA Ops:
  0.0 19.4 %shard_map.55 = f32[8,64,1024]{2,1,0:T(8,128)S(1)} custom-call(f32[8,64,1024]{2,1,0:T(8,128)} %bitcast.7, f32[8,64,1024]{2,1,0:T(8,128)} %bitcast.8, f32[8,64,1024]{2,1,0:T(8,128)} %bitcast.9, f32[8,64,1024]{2,1,0:T(8,128)} %bitcast.10, f32[8,64,1024]{2,1,0:T(8,128)} %bitcast.11), custom_call_target="tpu_custom_call" | custom-call | flops 47185920 | bytes 12582912 | tf_op jit(solution)/shard_map/pallas_call | solution.py:347
  19.4 1.3 %copy.7 = f32[512,1024]{1,0:T(8,128)} copy(f32[512,1024]{1,0:T(8,128)S(1)} %bitcast.6) | data formatting | bytes 4194304

commit v3 on v2

--- a/solution.py
+++ b/solution.py
@@ -154,8 +154,39 @@
     def packed(tile):
         return pl.ds(tile * SUB, SUB)
 
+    def outward(peer, source):
+        return pltpu.make_async_remote_copy(
+            src_ref=send_s.at[peer],
+            dst_ref=recv_s.at[pl.ds(pl.multiple_of(source * SENT, SENT), SENT), :],
+            send_sem=send_sem.at[peer],
+            recv_sem=recv_sem.at[source],
+            device_id={"lon": peer},
+            device_id_type=pl.DeviceIdType.MESH,
+        )
+
+    def homeward(peer, source):
+        return pltpu.make_async_remote_copy(
+            src_ref=back_s.at[pl.ds(pl.multiple_of(peer * BACK, BACK), BACK), :],
+            dst_ref=ret_s.at[source],
+            send_sem=back_send_sem.at[peer],
+            recv_sem=back_recv_sem.at[source],
+            device_id={"lon": peer},
+            device_id_type=pl.DeviceIdType.MESH,
+        )
+
+    def whole(tile, carry):
+        piece = tuple(piece_s[tile, pl.ds(idx * SUB, SUB), :] for idx in range(20))
+        for level in range(LEVELS):
+            piece, meet = joined(piece, rolled(piece, -(1 << level)))
+            for idx, value in enumerate(meet):
+                inner_s[tile, pl.ds((level * 20 + idx) * SUB, SUB), :] = value
+        for idx, value in enumerate(piece):
+            send_s[tile, pl.ds(idx, 1), :] = value[0:1, :]
+        return carry
+
     for base in range(0, tiles, group):
         members = list(range(base, base + group))
+
         def forward(i, state, members=members):
             new_state = []
             for tile, (p1, q1, g1, a1, b1, p2, q2, g2, a2, b2) in zip(members, state):
@@ -188,7 +219,7 @@
                 for copy in loads(tile, part):
                     copy.wait()
             span = length // PARTS
-            ends = lax.fori_loop(part * span, (part + 1) * span, forward, ends, unroll=2)
+            ends = lax.fori_loop(part * span, (part + 1) * span, forward, ends, unroll=4)
 
         def first_rows(i, state, members=members):
             new_state = []
@@ -203,7 +234,7 @@
             return tuple(new_state)
 
         forms = ((zero, one, zero, zero, zero), (zero, zero, one, zero, zero))
-        firsts = lax.fori_loop(0, length, first_rows, (forms,) * group, unroll=2)
+        firsts = lax.fori_loop(0, length, first_rows, (forms,) * group, unroll=8)
 
         for tile, end, (f0, f1) in zip(members, ends, firsts):
             p1, q1, g1, a1, b1, p2, q2, g2, a2, b2 = end
@@ -218,41 +249,11 @@
             for idx, value in enumerate(piece):
                 piece_s[tile, pl.ds(idx * SUB, SUB), :] = value
 
-    def whole(tile, carry):
-        piece = tuple(piece_s[tile, pl.ds(idx * SUB, SUB), :] for idx in range(20))
-        for level in range(LEVELS):
-            piece, meet = joined(piece, rolled(piece, -(1 << level)))
-            for idx, value in enumerate(meet):
-                inner_s[tile, pl.ds((level * 20 + idx) * SUB, SUB), :] = value
-        for idx, value in enumerate(piece):
-            send_s[tile, pl.ds(idx, 1), :] = value[0:1, :]
-        return carry
-
-    lax.fori_loop(0, tiles, whole, 0, unroll=2)
-
-    def outward(peer, source):
-        return pltpu.make_async_remote_copy(
-            src_ref=send_s.at[peer],
-            dst_ref=recv_s.at[pl.ds(pl.multiple_of(source * SENT, SENT), SENT), :],
-            send_sem=send_sem.at[peer],
-            recv_sem=recv_sem.at[source],
-            device_id={"lon": peer},
-            device_id_type=pl.DeviceIdType.MESH,
-        )
-
-    def homeward(peer, source):
-        return pltpu.make_async_remote_copy(
-            src_ref=back_s.at[pl.ds(pl.multiple_of(peer * BACK, BACK), BACK), :],
-            dst_ref=ret_s.at[source],
-            send_sem=back_send_sem.at[peer],
-            recv_sem=back_recv_sem.at[source],
-            device_id={"lon": peer},
-            device_id_type=pl.DeviceIdType.MESH,
-        )
-
-    pl.semaphore_wait(barrier, peers - 1)
-    for peer in others:
-        owning(peer, lambda peer=peer: outward(peer, me).start())
+        lax.fori_loop(base, base + group, whole, 0, unroll=2)
+        if base == 0:
+            pl.semaphore_wait(barrier, peers - 1)
+        for tile in members:
+            pl.when(me != tile)(lambda tile=tile: outward(tile, me).start())
 
     def solve_lines():
         recv_s[pl.ds(pl.multiple_of(me * SENT, SENT), SENT), :] = send_s[me]
@@ -280,19 +281,19 @@
 
     owning(me, solve_lines)
 
-    for peer in others:
-        owning(peer, lambda peer=peer: homeward(me, peer).wait_recv())
-
-    def store(tile):
+    def store(tile, part):
+        some = pl.ds(part * (length // PARTS), length // PARTS)
         return pltpu.make_async_copy(
-            z_s.at[pl.ds(tile * SUB, SUB), pl.ds(0, length), :],
-            z_hbm.at[:, :, pl.ds(tile * LANE, LANE)],
-            out_sem.at[tile],
+            z_s.at[pl.ds(tile * SUB, SUB), some, :],
+            z_hbm.at[:, some, pl.ds(tile * LANE, LANE)],
+            out_sem.at[tile, part],
         )
 
     for base in range(0, tiles, group):
         members = list(range(base, base + group))
         start, bounds = [], []
+        for tile in members:
+            pl.when(me != tile)(lambda tile=tile: homeward(me, tile).wait_recv())
         for tile in members:
             e0, e1, w0, w1 = (
                 jnp.broadcast_to(ret_s[tile, pl.ds(idx, 1), :], (SUB, LANE)) for idx in range(4)
@@ -317,14 +318,19 @@
                 new_state.append((x0, x1))
             return tuple(new_state)
 
-        lax.fori_loop(0, length, backward, tuple(start), unroll=2)
-        for tile in members:
-            store(tile).start()
+        state = tuple(start)
+        for part in reversed(range(PARTS)):
+            span = length // PARTS
+            done = (PARTS - 1 - part) * span
+            state = lax.fori_loop(done, done + span, backward, state, unroll=8)
+            for tile in members:
+                store(tile, part).start()
 
     for tile in range(tiles):
-        store(tile).wait()
-    for peer in others:
-        owning(peer, lambda peer=peer: outward(peer, me).wait_send())
+        for part in range(PARTS):
+            store(tile, part).wait()
+    for tile in range(tiles):
+        pl.when(me != tile)(lambda tile=tile: outward(tile, me).wait_send())
 
     def sent_home():
         for peer in others:
@@ -359,7 +365,7 @@
             pltpu.VMEM((peers * BACK, LANE), F32),
             pltpu.VMEM((tiles, BACK, LANE), F32),
             sem((5, tiles, PARTS)),
-            sem((tiles,)),
+            sem((tiles, PARTS)),
             sem((peers,)),
             sem((peers,)),
             sem((peers,)),

time: 20.9 us -> 18.7 us (0.89)
  Pallas kernels: 19.4 us -> 17.2 us
    pallas_call x1, Pallas kernels: 19.4 us -> 17.2 us  [per_device(): pl.pallas_call(functools.partial(kernel, peers), out_shape=jax.ShapeDtype...]
where the time goes in v3:
time: 18.7 us; the launch traced here: 18.6 us
  Pallas kernels  17.2 us (92%)
  local copies, waits for them, and re-layouts  1.32 us (7%)
    pallas_call x1, Pallas kernels, per_device(): pl.pallas_call(functools.partial(kernel, peers), out_shape=jax.ShapeDtype...  17.2 us
    unnamed x1, local copies, waits for them, and re-layouts  1.32 us

profile of v3, /device:TPU:0, one launch (start us, length us, event | category | flops | bytes accessed | tf_op | source)
XLA Modules:
  0.0 18.6 jit_solution(17322799823000320551)
XLA Ops:
  0.0 17.2 %shard_map.55 = f32[8,64,1024]{2,1,0:T(8,128)S(1)} custom-call(f32[8,64,1024]{2,1,0:T(8,128)} %bitcast.7, f32[8,64,1024]{2,1,0:T(8,128)} %bitcast.8, f32[8,64,1024]{2,1,0:T(8,128)} %bitcast.9, f32[8,64,1024]{2,1,0:T(8,128)} %bitcast.10, f32[8,64,1024]{2,1,0:T(8,128)} %bitcast.11), custom_call_target="tpu_custom_call" | custom-call | flops 47185920 | bytes 12582912 | tf_op jit(solution)/shard_map/pallas_call | solution.py:353
  17.2 1.3 %copy.7 = f32[512,1024]{1,0:T(8,128)} copy(f32[512,1024]{1,0:T(8,128)S(1)} %bitcast.6) | data formatting | bytes 4194304

commit v4 on v3

--- a/solution.py
+++ b/solution.py
@@ -126,16 +126,18 @@
             for idx, (src, dst) in enumerate(pairs)
         ]
 
-    flat_rows = tiles * SUB * pitch
+    flat_rows = (tiles + 1) * SUB * pitch
     t_f, l2_f, l1_f, u1_f, u2_f, z_f = (
         ref.reshape(flat_rows, LANE) for ref in (t_s, l2_s, l1_s, u1_s, u2_s, z_s)
     )
 
-    for base in range(0, tiles, group):
+    def start_loads(base):
         for part in range(PARTS):
             for tile in range(base, base + group):
                 for copy in loads(tile, part):
                     copy.start()
+
+    start_loads(0)
 
     barrier = pltpu.get_barrier_semaphore()
     for peer in others:
@@ -220,6 +222,8 @@
                     copy.wait()
             span = length // PARTS
             ends = lax.fori_loop(part * span, (part + 1) * span, forward, ends, unroll=4)
+            if part == 0 and base + group < tiles:
+                start_loads(base + group)
 
         def first_rows(i, state, members=members):
             new_state = []
@@ -347,7 +351,7 @@
     assert tiles % min(GROUP, tiles) == 0
     length = rows // SUB
     pitch = length if length % (2 * SUB) else length + SUB
-    plane = pltpu.VMEM((tiles * SUB, pitch, LANE), F32)
+    plane = pltpu.VMEM(((tiles + 1) * SUB, pitch, LANE), F32)
     factor = pltpu.VMEM((length, tiles * SUB, LANE), F32)
     sem = pltpu.SemaphoreType.DMA
     solved = pl.pallas_call(
@@ -361,8 +365,8 @@
             pltpu.VMEM((tiles, 20 * SUB, LANE), F32),
             pltpu.VMEM((tiles, LEVELS * 20 * SUB, LANE), F32),
             pltpu.VMEM((tiles, SENT, LANE), F32),
-            pltpu.VMEM((peers * SENT, LANE), F32),
-            pltpu.VMEM((peers * BACK, LANE), F32),
+            pltpu.VMEM(((peers + 1) * SENT, LANE), F32),
+            pltpu.VMEM(((peers + 1) * BACK, LANE), F32),
             pltpu.VMEM((tiles, BACK, LANE), F32),
             sem((5, tiles, PARTS)),
             sem((tiles, PARTS)),

time: 18.7 us -> 18.9 us (1.011)
  Pallas kernels: 17.2 us -> 17.4 us
where the time goes in v4:
time: 18.9 us; the launch traced here: 18.7 us
  Pallas kernels  17.4 us (92%)
  local copies, waits for them, and re-layouts  1.32 us (7%)
    pallas_call x1, Pallas kernels, per_device(): pl.pallas_call(functools.partial(kernel, peers), out_shape=jax.ShapeDtype...  17.4 us
    unnamed x1, local copies, waits for them, and re-layouts  1.32 us

profile of v4, /device:TPU:0, one launch (start us, length us, event | category | flops | bytes accessed | tf_op | source)
XLA Modules:
  0.0 18.7 jit_solution(16824225024967474572)
XLA Ops:
  0.0 17.4 %shard_map.55 = f32[8,64,1024]{2,1,0:T(8,128)S(1)} custom-call(f32[8,64,1024]{2,1,0:T(8,128)} %bitcast.7, f32[8,64,1024]{2,1,0:T(8,128)} %bitcast.8, f32[8,64,1024]{2,1,0:T(8,128)} %bitcast.9, f32[8,64,1024]{2,1,0:T(8,128)} %bitcast.10, f32[8,64,1024]{2,1,0:T(8,128)} %bitcast.11), custom_call_target="tpu_custom_call" | custom-call | flops 47185920 | bytes 12582912 | tf_op jit(solution)/shard_map/pallas_call | solution.py:357
  17.4 1.3 %copy.7 = f32[512,1024]{1,0:T(8,128)} copy(f32[512,1024]{1,0:T(8,128)S(1)} %bitcast.6) | data formatting | bytes 4194304

commit v5 on v4

--- a/solution.py
+++ b/solution.py
@@ -191,7 +191,8 @@
 
         def forward(i, state, members=members):
             new_state = []
-            for tile, (p1, q1, g1, a1, b1, p2, q2, g2, a2, b2) in zip(members, state):
+            for tile, (rows_state, forms) in zip(members, state):
+                p1, q1, g1, a1, b1, p2, q2, g2, a2, b2 = rows_state
                 here = strided(tile, i)
                 l2, l1, u1, u2 = l2_f[here, :], l1_f[here, :], u1_f[here, :], u2_f[here, :]
                 target = t_f[here, :]
@@ -211,11 +212,16 @@
                 g_s[i, at, :] = g0
                 wa_s[i, at, :] = a0
                 wb_s[i, at, :] = b0
-                new_state.append((p0, q0, g0, a0, b0, p1, q1, g1, a1, b1))
+                new_forms = tuple(
+                    (c + x * g0, y + x * p0, x * q0, a + x * a0, b + x * b0)
+                    for c, x, y, a, b in forms
+                )
+                new_state.append(((p0, q0, g0, a0, b0, p1, q1, g1, a1, b1), new_forms))
             return tuple(new_state)
 
         start = (zero, zero, zero, zero, one, zero, zero, zero, one, zero)
-        ends = (start,) * group
+        forms = ((zero, one, zero, zero, zero), (zero, zero, one, zero, zero))
+        ends = ((start, forms),) * group
         for part in range(PARTS):
             for tile in members:
                 for copy in loads(tile, part):
@@ -225,22 +231,7 @@
             if part == 0 and base + group < tiles:
                 start_loads(base + group)
 
-        def first_rows(i, state, members=members):
-            new_state = []
-            for tile, forms in zip(members, state):
-                at = packed(tile)
-                p, q, g = p_s[i, at, :], q_s[i, at, :], g_s[i, at, :]
-                wa, wb = wa_s[i, at, :], wb_s[i, at, :]
-                new_forms = []
-                for c, x, y, a, b in forms:
-                    new_forms.append((c + x * g, y + x * p, x * q, a + x * wa, b + x * wb))
-                new_state.append(tuple(new_forms))
-            return tuple(new_state)
-
-        forms = ((zero, one, zero, zero, zero), (zero, zero, one, zero, zero))
-        firsts = lax.fori_loop(0, length, first_rows, (forms,) * group, unroll=8)
-
-        for tile, end, (f0, f1) in zip(members, ends, firsts):
+        for tile, (end, (f0, f1)) in zip(members, ends):
             p1, q1, g1, a1, b1, p2, q2, g2, a2, b2 = end
             piece = (
                 f0[0], f1[0],

time: 18.9 us -> 19.9 us (1.053)
  Pallas kernels: 17.4 us -> 18.4 us
    pallas_call x1, Pallas kernels: 17.4 us -> 18.4 us  [per_device(): pl.pallas_call(functools.partial(kernel, peers), out_shape=jax.ShapeDtype...]
where the time goes in v5:
time: 19.9 us; the launch traced here: 19.8 us
  Pallas kernels  18.4 us (92%)
  local copies, waits for them, and re-layouts  1.32 us (7%)
    pallas_call x1, Pallas kernels, per_device(): pl.pallas_call(functools.partial(kernel, peers), out_shape=jax.ShapeDtype...  18.4 us
    unnamed x1, local copies, waits for them, and re-layouts  1.32 us

profile of v5, /device:TPU:0, one launch (start us, length us, event | category | flops | bytes accessed | tf_op | source)
XLA Modules:
  0.0 19.8 jit_solution(4213999219435396865)
XLA Ops:
  0.0 18.4 %shard_map.55 = f32[8,64,1024]{2,1,0:T(8,128)S(1)} custom-call(f32[8,64,1024]{2,1,0:T(8,128)} %bitcast.7, f32[8,64,1024]{2,1,0:T(8,128)} %bitcast.8, f32[8,64,1024]{2,1,0:T(8,128)} %bitcast.9, f32[8,64,1024]{2,1,0:T(8,128)} %bitcast.10, f32[8,64,1024]{2,1,0:T(8,128)} %bitcast.11), custom_call_target="tpu_custom_call" | custom-call | flops 47185920 | bytes 12582912 | tf_op jit(solution)/shard_map/pallas_call | solution.py:348
  18.4 1.3 %copy.7 = f32[512,1024]{1,0:T(8,128)} copy(f32[512,1024]{1,0:T(8,128)S(1)} %bitcast.6) | data formatting | bytes 4194304

commit v6 on v4

--- a/solution.py
+++ b/solution.py
@@ -221,7 +221,7 @@
                 for copy in loads(tile, part):
                     copy.wait()
             span = length // PARTS
-            ends = lax.fori_loop(part * span, (part + 1) * span, forward, ends, unroll=4)
+            ends = lax.fori_loop(part * span, (part + 1) * span, forward, ends, unroll=min(8, span))
             if part == 0 and base + group < tiles:
                 start_loads(base + group)
 
@@ -238,7 +238,7 @@
             return tuple(new_state)
 
         forms = ((zero, one, zero, zero, zero), (zero, zero, one, zero, zero))
-        firsts = lax.fori_loop(0, length, first_rows, (forms,) * group, unroll=8)
+        firsts = lax.fori_loop(0, length, first_rows, (forms,) * group, unroll=min(16, length))
 
         for tile, end, (f0, f1) in zip(members, ends, firsts):
             p1, q1, g1, a1, b1, p2, q2, g2, a2, b2 = end
@@ -326,7 +326,7 @@
         for part in reversed(range(PARTS)):
             span = length // PARTS
             done = (PARTS - 1 - part) * span
-            state = lax.fori_loop(done, done + span, backward, state, unroll=8)
+            state = lax.fori_loop(done, done + span, backward, state, unroll=min(16, span))
             for tile in members:
                 store(tile, part).start()
 

time: 18.9 us -> 18.7 us (0.989)
  no operation moved by 1% of the time
where the time goes in v6:
time: 18.7 us; the launch traced here: 18.6 us
  Pallas kernels  17.3 us (93%)
  local copies, waits for them, and re-layouts  1.32 us (7%)
    pallas_call x1, Pallas kernels, per_device(): pl.pallas_call(functools.partial(kernel, peers), out_shape=jax.ShapeDtype...  17.3 us
    unnamed x1, local copies, waits for them, and re-layouts  1.32 us

profile of v6, /device:TPU:0, one launch (start us, length us, event | category | flops | bytes accessed | tf_op | source)
XLA Modules:
  0.0 18.6 jit_solution(1221150606867911951)
XLA Ops:
  0.0 17.3 %shard_map.55 = f32[8,64,1024]{2,1,0:T(8,128)S(1)} custom-call(f32[8,64,1024]{2,1,0:T(8,128)} %bitcast.7, f32[8,64,1024]{2,1,0:T(8,128)} %bitcast.8, f32[8,64,1024]{2,1,0:T(8,128)} %bitcast.9, f32[8,64,1024]{2,1,0:T(8,128)} %bitcast.10, f32[8,64,1024]{2,1,0:T(8,128)} %bitcast.11), custom_call_target="tpu_custom_call" | custom-call | flops 47185920 | bytes 12582912 | tf_op jit(solution)/shard_map/pallas_call | solution.py:357
  17.3 1.3 %copy.7 = f32[512,1024]{1,0:T(8,128)} copy(f32[512,1024]{1,0:T(8,128)S(1)} %bitcast.6) | data formatting | bytes 4194304
